TPU v7x, 32 devices: a whole 2x2x4 slice. The times are simulated.
32 devices in a mesh: grp: 2 (over y), gz: 4 (over z), phi: 4 (over x, core).
Axes of the slice: x: 2, y: 2, z: 4, core: 2. Of those that a mesh axis runs over, the one named last changes fastest.
Arguments:
- charge: bfloat16 [2048, 128, 256], P(('grp', 'phi'), 'gz'), parts along dimension 0, may hold values from -44 to 44
- orders: int32 [64], replicated, may hold values from 1 to 255, as said below
- electrode: int32 [128, 256], P('gz'), may hold values 0 or 1
Outputs:
- distortion: bfloat16 [2048, 128, 256], P(('grp', 'phi'), 'gz'), parts along dimension 0
- potential: float32 [256, 128, 256], P(('grp', 'phi'), 'gz'), parts along dimension 0
There are 2 independent parts, one for each index of `grp`. A program takes and returns all parts, laid end to end along the dimension named above; an argument that names none is the same for every part. Nothing has to cross between parts.
Inputs may be any that keep to these rules, and one draw needn't show every extreme that they name: The 64 orders are distinct, and 1 and 255 are among them.
All inputs are finite; a program needn't handle non-finite values. No bound on the sum of `electrode` on one device may be relied on, other than what follows from the above.
Results may differ from a plain program's by a relative error of at most 0.0059.
Values may be sent and summed in bfloat16 or wider, within the bound.
A program may use at most 64 MiB of HBM per device.

v0:
```python
import math

import jax
import jax.numpy as jnp
from jax import lax
from jax.sharding import PartitionSpec as P

PHI = 1024
ORDERS = 64
MODES = 128
SWEEPS = 4


def with_halo(array, sides, width):
    for axis, dim in sides:
        count, length = (lax.axis_size(axis), array.shape[dim])
        up = [(i, (i + 1) % count) for i in range(count - 1)]
        down = [(j, i) for i, j in up]
        last = lax.slice_in_dim(array, length - width, length, axis=dim)
        first = lax.slice_in_dim(array, 0, width, axis=dim)
        before = lax.ppermute(last, axis, up)
        after = lax.ppermute(first, axis, down)
        array = jnp.concatenate([before, array, after], axis=dim)
    return array


def passed_along(block, axis, distance):
    devices = range(lax.axis_size(axis))
    route = [(i - distance, i) for i in devices if i - distance in devices]
    return lax.ppermute(block, axis, route)


def make_table(orders):
    positions = jnp.arange(PHI, dtype=jnp.int32)
    phase_int = orders[:, None] * positions[None, :] % PHI
    angles = phase_int.astype(jnp.float32) * (2.0 * math.pi / PHI)
    return jnp.concatenate([jnp.cos(angles), jnp.sin(angles)], 0).astype(jnp.bfloat16)


def radial_terms(order_values, radial_cells):
    radius = jnp.arange(radial_cells, dtype=jnp.float32) + (radial_cells // 2 + 0.5)
    outer_coef = 1.0 + 0.5 / radius
    inner_coef = 1.0 - 0.5 / radius
    diagonal = 4.0 + (order_values[:, None] / radius[None, :]) ** 2
    return (outer_coef, inner_coef, diagonal[:, None, :])


def radial_sum(field_now, outer_coef, inner_coef):
    zero_plane = jnp.zeros_like(field_now[..., :1])
    upper_cell = jnp.concatenate([field_now[..., 1:], zero_plane], -1)
    lower_cell = jnp.concatenate([zero_plane, field_now[..., :-1]], -1)
    return (outer_coef * upper_cell + inner_coef * lower_cell, upper_cell, lower_cell)


def on_device(charge, orders, electrode):
    phi_rows, slab_depth, radial_cells = charge.shape
    mode_rows = MODES // lax.axis_size("phi")
    slab_count = lax.axis_size("gz")
    basis_table = make_table(orders)
    local_cols = lax.dynamic_slice_in_dim(
        basis_table, lax.axis_index("phi") * phi_rows, phi_rows, 1
    )
    flattened = charge.reshape(phi_rows, slab_depth * radial_cells)
    summed = lax.psum_scatter(
        jnp.dot(local_cols, flattened, preferred_element_type=jnp.float32),
        "phi",
        scatter_dimension=0,
        tiled=True,
    )
    source = summed.reshape(mode_rows, slab_depth, radial_cells) * PHI ** (-0.5)
    mode_ids = lax.axis_index("phi") * mode_rows + jnp.arange(mode_rows, dtype=jnp.int32)
    matches = mode_ids[:, None] % ORDERS == jnp.arange(ORDERS, dtype=jnp.int32)[None, :]
    order_values = jnp.sum(jnp.where(matches, orders[None, :], 0), 1).astype(jnp.float32)
    outer_coef, inner_coef, diagonal = radial_terms(order_values, radial_cells)
    open_cells = (1 - electrode).astype(jnp.float32)
    stacked = jnp.concatenate([source, open_cells[None]], 0)
    widened = with_halo(stacked, (("gz", 1),), SWEEPS)
    wide_source = widened[:mode_rows]
    wide_open = widened[mode_rows]
    potential = wide_open * wide_source / diagonal
    for sweep in range(SWEEPS):
        zero_plane = jnp.zeros_like(potential[:, :1])
        upper_plane = jnp.concatenate([potential[:, 1:], zero_plane], 1)
        lower_plane = jnp.concatenate([zero_plane, potential[:, :-1]], 1)
        radial, _, _ = radial_sum(potential, outer_coef, inner_coef)
        neighbours = upper_plane + lower_plane + radial
        potential = wide_open * (wide_source + neighbours) / diagonal
    potential = potential[:, SWEEPS : SWEEPS + slab_depth]
    _, upper_cell, lower_cell = radial_sum(potential, outer_coef, inner_coef)
    radial_field = 0.5 * (upper_cell - lower_cell)
    local_sum = lax.cumsum(radial_field, axis=1, reverse=True)
    totals = local_sum[:, 0]

    def relay(step_index, incoming):
        return passed_along(totals + incoming, "gz", -1)

    incoming = lax.fori_loop(0, slab_count - 1, relay, jnp.zeros_like(totals))
    mode_shift = ((local_sum + incoming[:, None, :]) * (slab_count * slab_depth) ** (-0.5)).astype(
        jnp.bfloat16
    )
    weights_all = local_cols.T
    shard_piece = lax.all_gather(mode_shift, "phi", axis=0, tiled=True)
    row_count = shard_piece.shape[0]
    running = jnp.dot(
        weights_all,
        shard_piece.reshape(row_count, slab_depth * radial_cells),
        preferred_element_type=jnp.float32,
    )
    distortion = (
        (running * MODES ** (-0.5)).astype(jnp.bfloat16).reshape(phi_rows, slab_depth, radial_cells)
    )
    return (distortion, potential)


def solution(mesh):
    return jax.shard_map(
        on_device,
        mesh=mesh,
        in_specs=(P(("grp", "phi"), "gz", None), P(), P("gz", None)),
        out_specs=(P(("grp", "phi"), "gz", None), P(("grp", "phi"), "gz", None)),
        check_vma=False,
    )
```

profile of v0, /device:TPU:0, one launch (start us, length us, event | category | flops | bytes accessed | tf_op | source)
XLA Modules:
  0.0 145.0 jit_solution(1187935521183579783)
XLA Ops:
  7.2 1.9 %sine_convert_fusion = (bf16[64,1024]{1,0:T(8,128)(2,1)S(1)}, bf16[64,1024]{1,0:T(8,128)(2,1)S(1)}) fusion(s32[64]{0:T(128)} %param.6), kind=kLoop, calls=%fused_computation.23 | loop fusion | flops 1048576 | bytes 262400 | tf_op jit(solution)/shard_map/convert.1
  9.1 8.5 %copy.10 = bf16[32,8,32,256]{3,1,2,0:T(8,128)(2,1)} copy(bf16[32,8,32,256]{3,2,1,0:T(8,128)(2,1)} %bitcast.25) | data formatting | bytes 8388608
  17.6 4.9 %fusion.12 = f32[128,8192]{1,0:T(8,128)} fusion(bf16[256,8192]{1,0:T(8,128)(2,1)} %bitcast.22, s32[]{:T(128)S(6)} %select_n.26, bf16[64,1024]{1,0:T(8,128)(2,1)S(1)} %get-tuple-element.47, bf16[64,1024]{1,0:T(8,128)(2,1)S(1)} %get-tuple-element.46), kind=kOutput, calls=%fused_computation.46 | convolution fusion | flops 537001984 | bytes 8650756 | tf_op jit(solution)/shard_map/dot_general | solution.py:65
  22.6 0.6 copy-done.1
  23.3 46.5 %reduce-scatter.2.cloned.1.call-done = f32[32,8192]{1,0:T(8,128)} async-done(((f32[128,8192]{1,0:T(8,128)}), f32[32,8192]{1,0:T(8,128)}) %reduce-scatter.2.cloned.1.call-update) | async-done | bytes 1048592 | tf_op jit(solution)/shard_map/reduce_scatter | solution.py:64
  69.9 1.3 broadcast_multiply_fusion
  71.6 3.4 %collective-permute-start.1 = (f32[33,4,256]{2,1,0:T(4,128)S(1)}, f32[33,4,256]{2,1,0:T(4,128)S(1)}, u32[]{:S(2)}, u32[]{:S(2)}) collective-permute-start(f32[33,4,256]{2,1,0:T(4,128)S(1)} %get-tuple-element.44), channel_id=1, source_target_pairs={{0,4},{4,8},{8,12},{1,5},{5,9},{9,13},{2,6},{6,10},{10,14},{3,7},{... | collective-permute-start | bytes 405512 | tf_op jit(solution)/shard_map/ppermute | solution.py:21
  75.0 1.5 %collective-permute-start.2 = (f32[33,4,256]{2,1,0:T(4,128)S(1)}, f32[33,4,256]{2,1,0:T(4,128)S(1)}, u32[]{:S(2)}, u32[]{:S(2)}) collective-permute-start(f32[33,4,256]{2,1,0:T(4,128)S(1)} %get-tuple-element.45), channel_id=1, source_target_pairs={{4,0},{8,4},{12,8},{5,1},{9,5},{13,9},{6,2},{10,6},{14,10},{7,3},{... | collective-permute-start | bytes 405512 | tf_op jit(solution)/shard_map/ppermute | solution.py:22
  76.5 1.3 collective-permute-done.1
  77.8 4.1 %collective-permute-done.2 = f32[33,4,256]{2,1,0:T(4,128)S(1)} collective-permute-done((f32[33,4,256]{2,1,0:T(4,128)S(1)}, f32[33,4,256]{2,1,0:T(4,128)S(1)}, u32[]{:S(2)}, u32[]{:S(2)}) %collective-permute-start.2) | collective-permute-done | bytes 135200 | tf_op jit(solution)/shard_map/ppermute | solution.py:22
  82.2 0.4 fusion.23
  82.8 0.9 multiply_divide_fusion.3
  83.7 0.4 fusion.21
  84.4 0.9 multiply_divide_fusion.2
  85.2 0.4 fusion.19
  85.9 0.9 multiply_divide_fusion.1
  86.8 0.4 fusion.17
  87.4 0.9 multiply_divide_fusion
  89.0 1.0 fusion.1
  90.1 17.4 %while.10 = (s32[]{:T(128)}, f32[32,256]{1,0:T(8,128)S(1)}, f32[32,256]{1,0:T(8,128)S(1)}, s32[]{:T(128)}) while((s32[]{:T(128)}, f32[32,256]{1,0:T(8,128)S(1)}, f32[32,256]{1,0:T(8,128)S(1)}, s32[]{:T(128)}) %tuple.34), condition=%wide.region_4.5_spmd, body=%wide.region_3.4_spmd.sunk | while | flops 8194 | bytes 229469 | solution.py:97
  90.1 1.3 collective-permute-start
  91.4 4.5 %collective-permute-done = f32[32,256]{1,0:T(8,128)S(1)} collective-permute-done((f32[32,256]{1,0:T(8,128)S(1)}, f32[32,256]{1,0:T(8,128)S(1)}, u32[]{:S(2)}, u32[]{:S(2)}) %collective-permute-start) | collective-permute-done | bytes 32800 | tf_op jit(solution)/shard_map/while/body/eval_jaxpr/ppermute | solution.py:30
  95.9 1.3 collective-permute-start
  97.2 4.5 %collective-permute-done = f32[32,256]{1,0:T(8,128)S(1)} collective-permute-done((f32[32,256]{1,0:T(8,128)S(1)}, f32[32,256]{1,0:T(8,128)S(1)}, u32[]{:S(2)}, u32[]{:S(2)}) %collective-permute-start) | collective-permute-done | bytes 32800 | tf_op jit(solution)/shard_map/while/body/eval_jaxpr/ppermute | solution.py:30
  101.7 1.3 collective-permute-start
  103.0 4.5 %collective-permute-done = f32[32,256]{1,0:T(8,128)S(1)} collective-permute-done((f32[32,256]{1,0:T(8,128)S(1)}, f32[32,256]{1,0:T(8,128)S(1)}, u32[]{:S(2)}, u32[]{:S(2)}) %collective-permute-start) | collective-permute-done | bytes 32800 | tf_op jit(solution)/shard_map/while/body/eval_jaxpr/ppermute | solution.py:30
  107.5 0.9 multiply_convert_fusion
  108.5 1.1 slice.117
  109.6 20.7 %all-gather.2.cloned.1.call-done = bf16[128,32,256]{2,0,1:T(8,128)(2,1)} async-done(((bf16[32,32,256]{2,0,1:T(8,128)(2,1)}), bf16[128,32,256]{2,0,1:T(8,128)(2,1)}) %all-gather.2.cloned.1.call-update) | async-done | bytes 2097168 | tf_op jit(solution)/shard_map/all_gather | solution.py:102
  130.3 3.2 %copy.9 = bf16[128,32,256]{0,2,1:T(8,128)(2,1)S(1)} copy(bf16[128,32,256]{2,0,1:T(8,128)(2,1)} %all-gather.2.cloned.1.call-done) | data formatting | bytes 4194304 | tf_op jit(solution)/shard_map/all_gather | solution.py:102
  133.5 1.3 fusion
  134.8 3.4 %copy.12 = bf16[32,8,32,256]{3,2,1,0:T(8,128)(2,1)} copy(bf16[32,8,32,256]{3,1,2,0:T(8,128)(2,1)S(1)} %bitcast.23) | data formatting | bytes 8388608
  (29 shorter events, 2.7 us)
Async XLA Ops:
  7.2 62.7 %reduce-scatter.2.cloned.1.call-start = ((), (), s32[]{:S(2)}) async-start(), calls=%async_computation.1 | async-start | bytes 5242880 | tf_op jit(solution)/shard_map/reduce_scatter | solution.py:64
  22.5 0.7 copy-start.1
  22.5 0.9 copy-start
  22.5 107.8 %all-gather.2.cloned.1.call-start = ((), (), s32[]{:S(2)}) async-start(), calls=%async_computation.2 | async-start | bytes 2621440 | tf_op jit(solution)/shard_map/all_gather | solution.py:102
  71.6 6.2 %collective-permute-start.1 = (f32[33,4,256]{2,1,0:T(4,128)S(1)}, f32[33,4,256]{2,1,0:T(4,128)S(1)}, u32[]{:S(2)}, u32[]{:S(2)}) collective-permute-start(f32[33,4,256]{2,1,0:T(4,128)S(1)} %get-tuple-element.44), channel_id=1, source_target_pairs={{0,4},{4,8},{8,12},{1,5},{5,9},{9,13},{2,6},{6,10},{10,14},{3,7},{... | collective-permute-start | bytes 405512 | tf_op jit(solution)/shard_map/ppermute | solution.py:21
  75.0 6.9 %collective-permute-start.2 = (f32[33,4,256]{2,1,0:T(4,128)S(1)}, f32[33,4,256]{2,1,0:T(4,128)S(1)}, u32[]{:S(2)}, u32[]{:S(2)}) collective-permute-start(f32[33,4,256]{2,1,0:T(4,128)S(1)} %get-tuple-element.45), channel_id=1, source_target_pairs={{4,0},{8,4},{12,8},{5,1},{9,5},{13,9},{6,2},{10,6},{14,10},{7,3},{... | collective-permute-start | bytes 405512 | tf_op jit(solution)/shard_map/ppermute | solution.py:22
  90.1 5.8 %collective-permute-start = (f32[32,256]{1,0:T(8,128)S(1)}, f32[32,256]{1,0:T(8,128)S(1)}, u32[]{:S(2)}, u32[]{:S(2)}) collective-permute-start(f32[32,256]{1,0:T(8,128)S(1)} %add.264), channel_id=1, source_target_pairs={{4,0},{8,4},{12,8},{5,1},{9,5},{13,9},{6,2},{10,6},{14,10},{7,3},{... | collective-permute-start | bytes 98312 | tf_op jit(solution)/shard_map/while/body/eval_jaxpr/ppermute | solution.py:30
  95.9 5.8 %collective-permute-start = (f32[32,256]{1,0:T(8,128)S(1)}, f32[32,256]{1,0:T(8,128)S(1)}, u32[]{:S(2)}, u32[]{:S(2)}) collective-permute-start(f32[32,256]{1,0:T(8,128)S(1)} %add.264), channel_id=1, source_target_pairs={{4,0},{8,4},{12,8},{5,1},{9,5},{13,9},{6,2},{10,6},{14,10},{7,3},{... | collective-permute-start | bytes 98312 | tf_op jit(solution)/shard_map/while/body/eval_jaxpr/ppermute | solution.py:30
  101.7 5.8 %collective-permute-start = (f32[32,256]{1,0:T(8,128)S(1)}, f32[32,256]{1,0:T(8,128)S(1)}, u32[]{:S(2)}, u32[]{:S(2)}) collective-permute-start(f32[32,256]{1,0:T(8,128)S(1)} %add.264), channel_id=1, source_target_pairs={{4,0},{8,4},{12,8},{5,1},{9,5},{13,9},{6,2},{10,6},{14,10},{7,3},{... | collective-permute-start | bytes 98312 | tf_op jit(solution)/shard_map/while/body/eval_jaxpr/ppermute | solution.py:30
Sparse Core Ops, SparseCore 0:
  22.6 47.2 reduce-scatter.1
  108.6 21.6 all-gather.1
where the time goes:
time: 145 us
  waiting for transfers between devices  86.1 us (59%)
  local copies, waits for them, and re-layouts  20.1 us (14%)
  between operations  14.3 us (10%)
  other arithmetic  9.56 us (7%)
  starting transfers between devices  8.8 us (6%)
  matrix products  6.15 us (4%)
    reduce_scatter x1, waiting for transfers between devices, on_device(): lax.psum_scatter(jnp.dot(local_cols, flattened, preferred_element_type=jn...  46.5 us
    all_gather x1, waiting for transfers between devices, on_device(): shard_piece = lax.all_gather(mode_shift, 'phi', axis=0, tiled=True)  20.7 us
    ppermute x3, waiting for transfers between devices, passed_along(): return lax.ppermute(block, axis, route)  13.5 us
    unnamed x7, local copies, waits for them, and re-layouts  12.8 us
    dot_general x1, matrix products, on_device(): jnp.dot(local_cols, flattened, preferred_element_type=jnp.float32)  4.86 us
    ppermute x1, waiting for transfers between devices, with_halo(): after = lax.ppermute(first, axis, down)  4.12 us
    ppermute x3, starting transfers between devices, passed_along(): return lax.ppermute(block, axis, route)  3.85 us
    div x4, other arithmetic, on_device(): potential = wide_open * (wide_source + neighbours) / diagonal  3.47 us
  transfers between devices with their start and end apart: 7, of which 7 were waited for; matrix products, arithmetic and copies ran while one was open for 1% of the time, Pallas kernels for 0%

commit v1 on v0

v1 whole, which is shorter than its diff:
```python
import functools
import math

import jax
import jax.numpy as jnp
from jax import lax
from jax.experimental import pallas as pl
from jax.experimental.pallas import tpu as pltpu
from jax.sharding import PartitionSpec as P

PHI = 1024
ORDERS = 64
MODES = 128
SWEEPS = 4
MESH = pl.DeviceIdType.MESH


def kernel(
    n, ngz, chunks, groups,
    basis_ref, ch_ref, open_ref, inv_ref, coef_ref,
    pot_ref, ms_ref,
    send1, keep, recv1, l2send, l2recv, openx, srcx, pa, pb, loc, tot, trecv,
    l1_s, l1_r, l2_s, l2_r, op_s, op_r, ha_s, ha_r, to_s, to_r, ag_s, ag_r, sb_s, sb_r, fw_s, fw_r,
):
    nq = n // 2
    depth, _, cells = ch_ref.shape
    rows = inv_ref.shape[1]
    mode_rows = chunks * rows
    zg = depth // groups
    h = SWEEPS
    me = lax.axis_index("phi")
    gz = lax.axis_index("gz")
    p, core = me // 2, lax.rem(me, 2)
    sib = p * 2 + 1 - core

    def remote(src, dst, s, r, where):
        return pltpu.make_async_remote_copy(
            src_ref=src, dst_ref=dst, send_sem=s, recv_sem=r, device_id=where, device_id_type=MESH
        )

    def quad(d):
        return lax.rem(p + d, nq)

    def slab(d):
        return lax.rem(gz + d, ngz)

    barrier = pltpu.get_barrier_semaphore()
    pl.semaphore_signal(barrier, inc=1, device_id={"phi": sib}, device_id_type=MESH)
    for d in range(1, nq):
        pl.semaphore_signal(
            barrier, inc=1, device_id={"phi": quad(d) * 2 + core}, device_id_type=MESH
        )
    for d in range(1, ngz):
        pl.semaphore_signal(barrier, inc=1, device_id={"gz": slab(d)}, device_id_type=MESH)

    def l1(c, g):
        part = (c, slice(None), pl.ds(g * zg, zg))
        return remote(send1.at[part], recv1.at[part], l1_s.at[c, g], l1_r.at[c, g], {"phi": sib})

    def l2(c, g, d):
        part = (c, d - 1, pl.ds(g * zg, zg))
        return remote(
            l2send.at[part], l2recv.at[part], l2_s.at[c, g, d - 1], l2_r.at[c, g, d - 1],
            {"phi": quad(d) * 2 + core},
        )

    def both_ways(action):
        @pl.when(gz > 0)
        def _():
            action(0, gz - 1)

        @pl.when(gz < ngz - 1)
        def _():
            action(1, gz + 1)

    def halo(buf_src, first, buf_dst, s, r, way, where):
        src = pl.ds(first, h) if way == 0 else pl.ds(first + depth - h, h)
        dst = pl.ds(h + depth, h) if way == 0 else pl.ds(0, h)
        return remote(buf_src.at[src], buf_dst.at[dst], s.at[way], r.at[way], {"gz": where})

    def halo_send(*args):
        both_ways(lambda way, where: halo(*args, way, where).start())

    def halo_wait_send(*args):
        both_ways(lambda way, where: halo(*args, way, where).wait_send())

    def halo_wait_recv(*args):
        both_ways(lambda way, where: halo(*args, 1 - way, where).wait_recv())

    def total(c, d):
        return remote(
            tot.at[c], trecv.at[c, d - 1], to_s.at[c, d - 1], to_r.at[c, d - 1], {"gz": slab(d)}
        )

    def block(owner, c):
        start = pl.multiple_of(owner * mode_rows + c * rows, rows)
        return ms_ref.at[:, pl.ds(start, rows), :]

    def gather(c, d):
        b = block(me, c)
        return remote(b, b, ag_s.at[c, d - 1], ag_r.at[c, d - 1], {"phi": quad(d) * 2 + core})

    def gather_sib(c):
        b = block(me, c)
        return remote(b, b, sb_s.at[c], sb_r.at[c], {"phi": sib})

    def forward(c, d):
        b = block(lax.rem(p - d + nq, nq) * 2 + core, c)
        return remote(b, b, fw_s.at[c, d - 1], fw_r.at[c, d - 1], {"phi": sib})

    openx[pl.ds(h, depth)] = open_ref[...]
    edge = jnp.zeros((h,) + srcx.shape[2:], jnp.float32)

    def no_slab(first):
        openx[pl.ds(first, h)] = jnp.zeros((h,) + openx.shape[1:], jnp.float32)
        for c in range(chunks):
            srcx[c, pl.ds(first, h)] = edge

    @pl.when(gz == 0)
    def _():
        no_slab(0)

    @pl.when(gz == ngz - 1)
    def _():
        no_slab(h + depth)

    pl.semaphore_wait(barrier, nq + ngz - 1)
    open_args = (open_ref, 0, openx, op_s, op_r)
    halo_send(*open_args)

    for g in range(groups):
        def plane(i, _, g=g):
            z = g * zg + i
            full = jnp.dot(basis_ref[...], ch_ref[z], preferred_element_type=jnp.float32)
            at = 0
            for buf in (send1, keep):
                for c in range(chunks):
                    for q in range(nq):
                        buf[c, q, z] = full[at : at + rows]
                        at += rows
            return 0

        lax.fori_loop(0, zg, plane, 0)
        for c in range(chunks):
            l1(c, g).start()

    for c in range(chunks):
        errors = tuple(jnp.zeros((rows, cells), jnp.float32) for _ in range(nq - 1))
        for g in range(groups):
            l1(c, g).wait_recv()

            def plane(i, errors, g=g, c=c):
                z = g * zg + i
                left = []
                for d in range(1, nq):
                    q = quad(d)
                    v = keep[c, q, z] + recv1[c, q, z] + errors[d - 1]
                    b = v.astype(jnp.bfloat16)
                    l2send[c, d - 1, z] = b
                    left.append(v - b.astype(jnp.float32))
                srcx[c, h + z] = keep[c, p, z] + recv1[c, p, z]
                return tuple(left)

            errors = lax.fori_loop(0, zg, plane, errors)
            for d in range(1, nq):
                l2(c, g, d).start()

    halo_wait_recv(*open_args)

    def outer(x):
        return pltpu.roll(x, cells - 1, x.ndim - 1)

    def inner(x):
        return pltpu.roll(x, 1, x.ndim - 1)

    c_out, c_in, f_out, f_in = (
        jnp.concatenate([coef_ref[i]] * (rows // 8), 0) for i in range(4)
    )

    def open_at(z, count):
        o = openx[pl.ds(z, count)]
        return jnp.concatenate([o] * (rows // 8), 1)

    for c in range(chunks):
        def gather_source(i, _, c=c):
            s = srcx[c, h + i]
            for d in range(1, nq):
                s = s + l2recv[c, d - 1, i].astype(jnp.float32)
            srcx[c, h + i] = s * PHI ** (-0.5)
            return 0

        for g in range(groups):
            for d in range(1, nq):
                l2(c, g, d).wait_recv()
            lax.fori_loop(g * zg, (g + 1) * zg, gather_source, 0)
        halo_args = (srcx.at[c], h, srcx.at[c], ha_s.at[c], ha_r.at[c])
        halo_send(*halo_args)
        halo_wait_recv(*halo_args)
        halo_wait_send(*halo_args)
        inv = inv_ref[c]

        def begin(i, _, c=c, inv=inv):
            z = i * 4
            pa[pl.ds(z, 4)] = open_at(z, 4) * inv * srcx[c, pl.ds(z, 4)]
            return 0

        lax.fori_loop(0, (depth + 2 * h) // 4, begin, 0)
        now, later = pa, pb
        for sweep in range(SWEEPS):
            first, length = sweep + 1, depth + 2 * (h - sweep - 1)
            step = 4 if length % 4 == 0 else 2

            def relax(i, _, c=c, inv=inv, now=now, later=later, first=first, step=step):
                z = first + i * step
                mid = now[pl.ds(z, step)]
                near = now[pl.ds(z + 1, step)] + now[pl.ds(z - 1, step)]
                near = near + (c_out * outer(mid) + c_in * inner(mid))
                new = open_at(z, step) * inv * (srcx[c, pl.ds(z, step)] + near)
                later[pl.ds(z, step)] = new
                return 0

            lax.fori_loop(0, length // step, relax, 0)
            now, later = later, now

        def suffix(i, acc, c=c, now=now):
            z = depth - 1 - i
            x = now[h + z]
            pot_ref[z, pl.ds(c * rows, rows)] = x
            acc = acc + (f_out * outer(x) - f_in * inner(x))
            loc[c, z] = acc
            return acc

        tot[c] = lax.fori_loop(0, depth, suffix, jnp.zeros((rows, cells), jnp.float32))
        for d in range(1, ngz):
            total(c, d).start()
        before = jnp.zeros((rows, cells), jnp.float32)
        for d in range(1, ngz):
            total(c, d).wait_recv()
            sender = lax.rem(gz - d + ngz, ngz)
            before = before + trecv[c, d - 1] * jnp.where(sender > gz, 1.0, 0.0)
        mine = pl.multiple_of(me * mode_rows + c * rows, rows)

        def shift(i, _, c=c, before=before, mine=mine):
            value = (loc[c, i] + before) * (ngz * depth) ** (-0.5)
            ms_ref[i, pl.ds(mine, rows), :] = value.astype(jnp.bfloat16)
            return 0

        lax.fori_loop(0, depth, shift, 0)
        for d in range(1, nq):
            gather(c, d).start()
        gather_sib(c).start()

    for c in range(chunks):
        for d in range(1, nq):
            gather(c, d).wait_recv()
            forward(c, d).start()
    for c in range(chunks):
        gather_sib(c).wait()
        for d in range(1, nq):
            gather(c, d).wait_send()
            forward(c, d).wait()
        for d in range(1, ngz):
            total(c, d).wait_send()
        for g in range(groups):
            l1(c, g).wait_send()
            for d in range(1, nq):
                l2(c, g, d).wait_send()
    halo_wait_send(*open_args)


def on_device(charge, orders, electrode):
    phi_rows, depth, cells = charge.shape
    n, ngz = lax.axis_size("phi"), lax.axis_size("gz")
    nq = n // 2
    mode_rows = MODES // n
    rows = 16 if mode_rows % 16 == 0 else mode_rows
    chunks = mode_rows // rows
    groups = 4
    me = lax.axis_index("phi")
    core = me % 2

    positions = me * phi_rows + jnp.arange(phi_rows, dtype=jnp.int32)
    phase_int = orders[:, None] * positions[None, :] % PHI
    angles = phase_int.astype(jnp.float32) * (2.0 * math.pi / PHI)
    table = jnp.concatenate([jnp.cos(angles), jnp.sin(angles)], 0).astype(jnp.bfloat16)
    blocks = table.reshape(nq, 2, chunks, rows, phi_rows)
    swapped = jnp.where(core == 0, blocks[:, ::-1], blocks)
    basis = swapped.transpose(1, 2, 0, 3, 4).reshape(MODES, phi_rows)

    mode_ids = me * mode_rows + jnp.arange(mode_rows, dtype=jnp.int32)
    matches = mode_ids[:, None] % ORDERS == jnp.arange(ORDERS, dtype=jnp.int32)[None, :]
    values = jnp.sum(jnp.where(matches, orders[None, :], 0), 1).astype(jnp.float32)
    cell = jnp.arange(cells, dtype=jnp.int32)
    radius = cell.astype(jnp.float32) + (cells // 2 + 0.5)
    inv = 1.0 / (4.0 + (values[:, None] / radius[None, :]) ** 2)
    inv = inv.reshape(chunks, rows, cells)
    not_last = (cell < cells - 1).astype(jnp.float32)
    not_first = (cell > 0).astype(jnp.float32)
    coef = jnp.stack(
        [
            (1.0 + 0.5 / radius) * not_last,
            (1.0 - 0.5 / radius) * not_first,
            0.5 * not_last,
            0.5 * not_first,
        ]
    )
    coef = jnp.broadcast_to(coef[:, None], (4, 8, cells))
    open_cells = (1 - electrode).astype(jnp.float32)
    open_cells = jnp.broadcast_to(open_cells[:, None], (depth, 8, cells))

    f32, bf16 = jnp.float32, jnp.bfloat16
    wide = depth + 2 * SWEEPS
    sem = pltpu.SemaphoreType.DMA
    vmem = pl.BlockSpec(memory_space=pltpu.VMEM)
    others = nq - 1
    potential, shifts = pl.pallas_call(
        functools.partial(kernel, n, ngz, chunks, groups),
        out_shape=(
            jax.ShapeDtypeStruct((depth, mode_rows, cells), f32),
            jax.ShapeDtypeStruct((depth, MODES, cells), bf16),
        ),
        in_specs=[vmem] * 5,
        out_specs=(vmem, vmem),
        scratch_shapes=[
            pltpu.VMEM((chunks, nq, depth, rows, cells), f32),
            pltpu.VMEM((chunks, nq, depth, rows, cells), f32),
            pltpu.VMEM((chunks, nq, depth, rows, cells), f32),
            pltpu.VMEM((chunks, others, depth, rows, cells), bf16),
            pltpu.VMEM((chunks, others, depth, rows, cells), bf16),
            pltpu.VMEM((wide, 8, cells), f32),
            pltpu.VMEM((chunks, wide, rows, cells), f32),
            pltpu.VMEM((wide, rows, cells), f32),
            pltpu.VMEM((wide, rows, cells), f32),
            pltpu.VMEM((chunks, depth, rows, cells), f32),
            pltpu.VMEM((chunks, rows, cells), f32),
            pltpu.VMEM((chunks, ngz - 1, rows, cells), f32),
            sem((chunks, groups)), sem((chunks, groups)),
            sem((chunks, groups, others)), sem((chunks, groups, others)),
            sem((2,)), sem((2,)),
            sem((chunks, 2)), sem((chunks, 2)),
            sem((chunks, ngz - 1)), sem((chunks, ngz - 1)),
            sem((chunks, others)), sem((chunks, others)),
            sem((chunks,)), sem((chunks,)),
            sem((chunks, others)), sem((chunks, others)),
        ],
        compiler_params=pltpu.CompilerParams(
            collective_id=0, has_side_effects=True, vmem_limit_bytes=48 * 1024 * 1024
        ),
    )(basis, charge.transpose(1, 0, 2), open_cells, inv, coef)

    running = jnp.einsum("mp,zmr->pzr", table, shifts, preferred_element_type=f32)
    distortion = (running * MODES ** (-0.5)).astype(bf16)
    return (distortion, potential.transpose(1, 0, 2))


def solution(mesh):
    return jax.shard_map(
        on_device,
        mesh=mesh,
        in_specs=(P(("grp", "phi"), "gz", None), P(), P("gz", None)),
        out_specs=(P(("grp", "phi"), "gz", None), P(("grp", "phi"), "gz", None)),
        check_vma=False,
    )
```

time: 145 us -> 76.4 us (0.53)
  waiting for transfers between devices: 86.1 us -> 0 us
  Pallas kernels: 0 us -> 58.2 us
  between operations: 14.3 us -> 0.75 us
  starting transfers between devices: 8.8 us -> 0 us
  local copies, waits for them, and re-layouts: 20.1 us -> 12.8 us
  other arithmetic: 9.56 us -> 3.1 us
  matrix products: 6.15 us -> 1.24 us
    pallas_call x0 -> x1, Pallas kernels: none -> 58.2 us  [on_device(): pl.pallas_call(functools.partial(kernel, n, ngz, chunks, groups), out_sha...]
    reduce_scatter x1 -> x0, waiting for transfers between devices: 46.5 us -> none  [on_device(): lax.psum_scatter(jnp.dot(local_cols, flattened, preferred_element_type=jn...]
    all_gather x1 -> x0, waiting for transfers between devices: 20.7 us -> none  [on_device(): shard_piece = lax.all_gather(mode_shift, 'phi', axis=0, tiled=True)]
    ppermute x5 -> x0, waiting for transfers between devices: 18.9 us -> none  [the longest x3 13.5 us: passed_along(): return lax.ppermute(block, axis, route)]
    ppermute x5 -> x0, starting transfers between devices: 8.72 us -> none  [the longest x3 3.85 us: passed_along(): return lax.ppermute(block, axis, route)]
    dot_general x2 -> x1, matrix products: 6.15 us -> 1.24 us  [on_device(): jnp.einsum('mp,zmr->pzr', table, shifts, preferred_element_type=f32)]
    slice x10 -> x0, local copies, waits for them, and re-layouts: 4.07 us -> none  [the longest x5 2.1 us: radial_sum(): upper_cell = jnp.concatenate([field_now[..., 1:], zero_plane], -1)]
    div x5 -> x1, other arithmetic: 3.74 us -> 0.08 us  [on_device(): inv = 1.0 / (4.0 + (values[:, None] / radius[None, :]) ** 2)]
  transfers between devices with their start and end apart: 7 -> 0, of which waited for: 7 -> 0; matrix products, arithmetic and copies ran while one was open for 1% -> 0% of each run, Pallas kernels for 0% -> 0%
where the time goes in v1:
time: 76.4 us; the launch traced here: 76.1 us
  Pallas kernels  58.2 us (76%)
  local copies, waits for them, and re-layouts  12.8 us (17%)
  other arithmetic  3.1 us (4%)
  matrix products  1.24 us (2%)
    pallas_call x1, Pallas kernels, on_device(): pl.pallas_call(functools.partial(kernel, n, ngz, chunks, groups), out_sha...  58.2 us
    unnamed x3, local copies, waits for them, and re-layouts  12.6 us

profile of v1, /device:TPU:0, one launch (start us, length us, event | category | flops | bytes accessed | tf_op | source)
XLA Modules:
  0.0 76.1 jit_solution(9558083160517716088)
XLA Ops:
  0.7 0.8 %select_reduce_fusion = s32[32]{0:T(128)S(1)} fusion(s32[64]{0:T(128)} %param.4, s32[32]{0:T(128)S(1)} %and_select_fusion), kind=kLoop, calls=%fused_computation.20 | loop fusion | flops 6112 | bytes 512 | tf_op jit(solution)/shard_map/reduce_sum | solution.py:292
  1.5 0.1 convert_element_type.54
  1.7 0.1 fusion.8.inv_ref
  1.8 0.8 %subtract_convert_fusion = f32[32,256]{1,0:T(8,128)S(1)} fusion(s32[32,256]{1,0:T(8,128)} %param.5), kind=kLoop, calls=%fused_computation.19 | loop fusion | flops 16384 | bytes 65536 | tf_op jit(solution)/shard_map/convert_element_type | solution.py:308
  2.5 1.2 %fusion.6 = (bf16[64,256]{0,1:T(8,128)(2,1)S(1)}, bf16[64,256]{0,1:T(8,128)(2,1)S(1)}) fusion(s32[256]{0:T(256)S(1)} %iota_add_fusion, s32[64]{0:T(128)} %param.4), kind=kLoop, calls=%fused_computation.15 | loop fusion | flops 262144 | bytes 66816 | tf_op jit(solution)/shard_map/cos | solution.py:285
  3.8 0.1 maximum_convert_fusion
  3.9 0.1 copy.15
  4.0 6.6 %copy.21 = bf16[256,32,256]{2,0,1:T(8,128)(2,1)} copy(bf16[256,32,256]{2,1,0:T(8,128)(2,1)} %param.3) | data formatting | bytes 8388608 | tf_op args[0]
  10.6 58.2 %shard_map.50 = (f32[32,32,256]{2,1,0:T(8,128)S(1)}, bf16[32,128,256]{2,1,0:T(8,128)(2,1)S(1)}) custom-call(bf16[128,256]{1,0:T(8,128)(2,1)S(1)} %bitcast.13, bf16[32,256,256]{2,1,0:T(8,128)(2,1)} %bitcast.14, f32[32,8,256]{2,1,0:T(8,128)S(1)} %broadcast_in_dim.16.open_ref, f32[2,16,256]{2,1,0:T(8,128)S(1)} %fusion.8.inv_ref, ...), custom_call_target="tpu_custom_call" | custom-call | tf_op jit(solution)/shard_map/pallas_call | solution.py:316
  68.8 1.6 %copy.19 = f32[32,32,256]{2,1,0:T(8,128)} copy(f32[32,32,256]{2,0,1:T(8,128)S(1)} %bitcast.12) | data formatting | bytes 2097152
  70.4 1.2 %multiply_convert_fusion = bf16[256,32,256]{2,0,1:T(8,128)(2,1)S(1)} fusion(bf16[32,128,256]{2,1,0:T(8,128)(2,1)S(1)} %get-tuple-element.4, bf16[128,256]{0,1:T(8,128)(2,1)S(1)} %maximum_convert_fusion), kind=kOutput, calls=%fused_computation | convolution fusion | flops 541065216 | bytes 6356992 | tf_op jit(solution)/shard_map/mp,zmr->pzr/dot_general | solution.py:351
  71.7 4.4 %copy.18 = bf16[256,32,256]{2,1,0:T(8,128)(2,1)} copy(bf16[256,32,256]{2,0,1:T(8,128)(2,1)S(1)} %multiply_convert_fusion) | data formatting | bytes 8388608
  (11 shorter events, 0.1 us)

commit v2 on v1

--- a/solution.py
+++ b/solution.py
@@ -19,7 +19,7 @@
     n, ngz, chunks, groups,
     basis_ref, ch_ref, open_ref, inv_ref, coef_ref,
     pot_ref, ms_ref,
-    send1, keep, recv1, l2send, l2recv, openx, srcx, pa, pb, loc, tot, trecv,
+    send1, keep, recv1, l2send, l2recv, openx, srcx, wx, pa, pb, loc, tot, trecv,
     l1_s, l1_r, l2_s, l2_r, op_s, op_r, ha_s, ha_r, to_s, to_r, ag_s, ag_r, sb_s, sb_r, fw_s, fw_r,
 ):
     nq = n // 2
@@ -140,7 +140,7 @@
                         at += rows
             return 0
 
-        lax.fori_loop(0, zg, plane, 0)
+        lax.fori_loop(0, zg, plane, 0, unroll=True)
         for c in range(chunks):
             l1(c, g).start()
 
@@ -161,7 +161,7 @@
                 srcx[c, h + z] = keep[c, p, z] + recv1[c, p, z]
                 return tuple(left)
 
-            errors = lax.fori_loop(0, zg, plane, errors)
+            errors = lax.fori_loop(0, zg, plane, errors, unroll=True)
             for d in range(1, nq):
                 l2(c, g, d).start()
 
@@ -192,7 +192,7 @@
         for g in range(groups):
             for d in range(1, nq):
                 l2(c, g, d).wait_recv()
-            lax.fori_loop(g * zg, (g + 1) * zg, gather_source, 0)
+            lax.fori_loop(g * zg, (g + 1) * zg, gather_source, 0, unroll=True)
         halo_args = (srcx.at[c], h, srcx.at[c], ha_s.at[c], ha_r.at[c])
         halo_send(*halo_args)
         halo_wait_recv(*halo_args)
@@ -201,25 +201,25 @@
 
         def begin(i, _, c=c, inv=inv):
             z = i * 4
-            pa[pl.ds(z, 4)] = open_at(z, 4) * inv * srcx[c, pl.ds(z, 4)]
+            weight = open_at(z, 4) * inv
+            wx[pl.ds(z, 4)] = weight
+            pa[pl.ds(z, 4)] = weight * srcx[c, pl.ds(z, 4)]
             return 0
 
-        lax.fori_loop(0, (depth + 2 * h) // 4, begin, 0)
+        lax.fori_loop(0, (depth + 2 * h) // 4, begin, 0, unroll=2)
         now, later = pa, pb
         for sweep in range(SWEEPS):
             first, length = sweep + 1, depth + 2 * (h - sweep - 1)
-            step = 4 if length % 4 == 0 else 2
-
-            def relax(i, _, c=c, inv=inv, now=now, later=later, first=first, step=step):
-                z = first + i * step
-                mid = now[pl.ds(z, step)]
-                near = now[pl.ds(z + 1, step)] + now[pl.ds(z - 1, step)]
+
+            def relax(i, _, c=c, now=now, later=later, first=first):
+                z = first + i
+                mid = now[z]
+                near = now[z + 1] + now[z - 1]
                 near = near + (c_out * outer(mid) + c_in * inner(mid))
-                new = open_at(z, step) * inv * (srcx[c, pl.ds(z, step)] + near)
-                later[pl.ds(z, step)] = new
+                later[z] = wx[z] * (srcx[c, z] + near)
                 return 0
 
-            lax.fori_loop(0, length // step, relax, 0)
+            lax.fori_loop(0, length, relax, 0, unroll=length // 2)
             now, later = later, now
 
         def suffix(i, acc, c=c, now=now):
@@ -230,7 +230,7 @@
             loc[c, z] = acc
             return acc
 
-        tot[c] = lax.fori_loop(0, depth, suffix, jnp.zeros((rows, cells), jnp.float32))
+        tot[c] = lax.fori_loop(0, depth, suffix, jnp.zeros((rows, cells), jnp.float32), unroll=8)
         for d in range(1, ngz):
             total(c, d).start()
         before = jnp.zeros((rows, cells), jnp.float32)
@@ -245,7 +245,7 @@
             ms_ref[i, pl.ds(mine, rows), :] = value.astype(jnp.bfloat16)
             return 0
 
-        lax.fori_loop(0, depth, shift, 0)
+        lax.fori_loop(0, depth, shift, 0, unroll=8)
         for d in range(1, nq):
             gather(c, d).start()
         gather_sib(c).start()
@@ -266,6 +266,21 @@
             for d in range(1, nq):
                 l2(c, g, d).wait_send()
     halo_wait_send(*open_args)
+
+
+def synthesize(weight_ref, shift_ref, out_ref, wide_ref):
+    for z in range(shift_ref.shape[0]):
+        wide_ref[:, z, :] = jnp.dot(
+            weight_ref[...], shift_ref[z], preferred_element_type=jnp.float32
+        )
+    step = 16
+
+    def narrow(i, _):
+        at = pl.ds(i * step, step)
+        out_ref[at] = (wide_ref[at] * MODES ** (-0.5)).astype(jnp.bfloat16)
+        return 0
+
+    lax.fori_loop(0, wide_ref.shape[0] // step, narrow, 0)
 
 
 def on_device(charge, orders, electrode):
@@ -331,6 +346,7 @@
             pltpu.VMEM((chunks, wide, rows, cells), f32),
             pltpu.VMEM((wide, rows, cells), f32),
             pltpu.VMEM((wide, rows, cells), f32),
+            pltpu.VMEM((wide, rows, cells), f32),
             pltpu.VMEM((chunks, depth, rows, cells), f32),
             pltpu.VMEM((chunks, rows, cells), f32),
             pltpu.VMEM((chunks, ngz - 1, rows, cells), f32),
@@ -348,8 +364,19 @@
         ),
     )(basis, charge.transpose(1, 0, 2), open_cells, inv, coef)
 
-    running = jnp.einsum("mp,zmr->pzr", table, shifts, preferred_element_type=f32)
-    distortion = (running * MODES ** (-0.5)).astype(bf16)
+    part = 16
+    distortion = pl.pallas_call(
+        synthesize,
+        grid=(depth // part,),
+        out_shape=jax.ShapeDtypeStruct((phi_rows, depth, cells), bf16),
+        in_specs=[
+            pl.BlockSpec((phi_rows, MODES), lambda i: (0, 0)),
+            pl.BlockSpec((part, MODES, cells), lambda i: (i, 0, 0)),
+        ],
+        out_specs=pl.BlockSpec((phi_rows, part, cells), lambda i: (0, i, 0)),
+        scratch_shapes=[pltpu.VMEM((phi_rows, part, cells), f32)],
+        compiler_params=pltpu.CompilerParams(vmem_limit_bytes=32 * 1024 * 1024),
+    )(table.T, shifts)
     return (distortion, potential.transpose(1, 0, 2))
 
 

time: 76.4 us -> 60.5 us (0.79)
  Pallas kernels: 58.2 us -> 47.9 us
  local copies, waits for them, and re-layouts: 12.8 us -> 8.37 us
  matrix products: 1.24 us -> 0 us
    pallas_call x1, Pallas kernels: 58.2 us -> 42.4 us  [on_device(): pl.pallas_call(functools.partial(kernel, n, ngz, chunks, groups), out_sha...]
    pallas_call x0 -> x1, Pallas kernels: none -> 5.53 us  [on_device(): pl.pallas_call(synthesize, grid=(depth // part,), out_shape=jax.ShapeDtyp...]
    unnamed x3 -> x2, local copies, waits for them, and re-layouts: 12.6 us -> 8.15 us
    dot_general x1 -> x0, matrix products: 1.24 us -> none  [on_device(): jnp.einsum('mp,zmr->pzr', table, shifts, preferred_element_type=f32)]
where the time goes in v2:
time: 60.5 us; the launch traced here: 60.2 us
  Pallas kernels  47.9 us (79%)
  local copies, waits for them, and re-layouts  8.37 us (14%)
  other arithmetic  3.19 us (5%)
  between operations  0.75 us (1%)
    pallas_call x1, Pallas kernels, on_device(): pl.pallas_call(functools.partial(kernel, n, ngz, chunks, groups), out_sha...  42.4 us
    unnamed x2, local copies, waits for them, and re-layouts  8.15 us
    pallas_call x1, Pallas kernels, on_device(): pl.pallas_call(synthesize, grid=(depth // part,), out_shape=jax.ShapeDtyp...  5.53 us
    cos x1, other arithmetic, on_device(): jnp.cos(angles)  1.25 us

profile of v2, /device:TPU:0, one launch (start us, length us, event | category | flops | bytes accessed | tf_op | source)
XLA Modules:
  0.0 60.2 jit_solution(13926663698527338403)
XLA Ops:
  0.7 0.8 %select_reduce_fusion = s32[32]{0:T(128)S(1)} fusion(s32[64]{0:T(128)} %param.4, s32[32]{0:T(128)S(1)} %and_select_fusion), kind=kLoop, calls=%fused_computation.18 | loop fusion | flops 6112 | bytes 512 | tf_op jit(solution)/shard_map/reduce_sum | solution.py:307
  1.5 0.1 convert_element_type.51
  1.7 0.1 fusion.7.inv_ref
  1.8 0.8 %subtract_convert_fusion = f32[32,256]{1,0:T(8,128)S(1)} fusion(s32[32,256]{1,0:T(8,128)} %param.5), kind=kLoop, calls=%fused_computation.17 | loop fusion | flops 16384 | bytes 65536 | tf_op jit(solution)/shard_map/convert_element_type | solution.py:323
  2.5 1.2 %fusion.5 = (bf16[64,256]{0,1:T(8,128)(2,1)S(1)}, bf16[64,256]{0,1:T(8,128)(2,1)S(1)}) fusion(s32[256]{0:T(256)S(1)} %iota_add_fusion, s32[64]{0:T(128)} %param.4), kind=kLoop, calls=%fused_computation.13 | loop fusion | flops 262144 | bytes 66816 | tf_op jit(solution)/shard_map/cos | solution.py:300
  3.8 0.1 fusion.9.weight_ref
  3.9 0.1 maximum_convert_fusion
  4.0 0.1 copy.12
  4.1 6.6 %copy.17 = bf16[256,32,256]{2,0,1:T(8,128)(2,1)} copy(bf16[256,32,256]{2,1,0:T(8,128)(2,1)} %param.3) | data formatting | bytes 8388608 | tf_op args[0]
  10.7 42.4 %shard_map.50 = (f32[32,32,256]{2,1,0:T(8,128)S(1)}, bf16[32,128,256]{2,1,0:T(8,128)(2,1)S(1)}) custom-call(bf16[128,256]{1,0:T(8,128)(2,1)S(1)} %bitcast.11, bf16[32,256,256]{2,1,0:T(8,128)(2,1)} %bitcast.12, f32[32,8,256]{2,1,0:T(8,128)S(1)} %broadcast_in_dim.16.open_ref, f32[2,16,256]{2,1,0:T(8,128)S(1)} %fusion.7.inv_ref, ...), custom_call_target="tpu_custom_call" | custom-call | tf_op jit(solution)/shard_map/pallas_call | solution.py:331
  53.1 1.6 %copy.15 = f32[32,32,256]{2,1,0:T(8,128)} copy(f32[32,32,256]{2,0,1:T(8,128)S(1)} %bitcast.10) | data formatting | bytes 2097152
  54.7 5.5 %shard_map.51 = bf16[256,32,256]{2,1,0:T(8,128)(2,1)} custom-call(bf16[256,128]{1,0:T(8,128)(2,1)S(1)} %fusion.9.weight_ref, bf16[32,128,256]{2,1,0:T(8,128)(2,1)S(1)} %get-tuple-element.4.shift_ref), custom_call_target="tpu_custom_call" | custom-call | tf_op jit(solution)/shard_map/pallas_call | solution.py:368
  (11 shorter events, 0.1 us)

commit v3 on v2

--- a/solution.py
+++ b/solution.py
@@ -17,13 +17,14 @@
 
 def kernel(
     n, ngz, chunks, groups,
-    basis_ref, ch_ref, open_ref, inv_ref, coef_ref,
+    basis_ref, charge_ref, open_ref, inv_ref, coef_ref,
     pot_ref, ms_ref,
-    send1, keep, recv1, l2send, l2recv, openx, srcx, wx, pa, pb, loc, tot, trecv,
+    ch, chf, ch_s, send1, keep, recv1, l2send, l2recv, openx, srcx, wx, pa, pb, loc, tot, trecv,
     l1_s, l1_r, l2_s, l2_r, op_s, op_r, ha_s, ha_r, to_s, to_r, ag_s, ag_r, sb_s, sb_r, fw_s, fw_r,
 ):
     nq = n // 2
-    depth, _, cells = ch_ref.shape
+    _, depth, cells = charge_ref.shape
+    part = ch.shape[2]
     rows = inv_ref.shape[1]
     mode_rows = chunks * rows
     zg = depth // groups
@@ -44,6 +45,12 @@
     def slab(d):
         return lax.rem(gz + d, ngz)
 
+    def load(j):
+        src = charge_ref.at[:, pl.ds(j * part, part), :]
+        return pltpu.make_async_copy(src, ch.at[j], ch_s.at[j])
+
+    for j in range(depth // part):
+        load(j).start()
     barrier = pltpu.get_barrier_semaphore()
     pl.semaphore_signal(barrier, inc=1, device_id={"phi": sib}, device_id_type=MESH)
     for d in range(1, nq):
@@ -128,10 +135,44 @@
     open_args = (open_ref, 0, openx, op_s, op_r)
     halo_send(*open_args)
 
+    def round_group(c, g, errors):
+        l1(c, g).wait_recv()
+
+        def plane(i, errors):
+            z = g * zg + i
+            left = []
+            for d in range(1, nq):
+                q = quad(d)
+                v = keep[c, q, z] + recv1[c, q, z] + errors[d - 1]
+                b = v.astype(jnp.bfloat16)
+                l2send[c, d - 1, z] = b
+                left.append(v - b.astype(jnp.float32))
+            srcx[c, h + z] = keep[c, p, z] + recv1[c, p, z]
+            return tuple(left)
+
+        errors = lax.fori_loop(0, zg, plane, errors, unroll=True)
+        for d in range(1, nq):
+            l2(c, g, d).start()
+        return errors
+
+    no_errors = tuple(jnp.zeros((rows, cells), jnp.float32) for _ in range(nq - 1))
+    errors = no_errors
     for g in range(groups):
-        def plane(i, _, g=g):
+        j = g * zg // part
+        if g * zg % part == 0:
+            load(j).wait()
+
+            def widen(i, _, j=j):
+                at = pl.ds(i * 8, 8)
+                chf[at] = ch[j, at].astype(jnp.float32)
+                return 0
+
+            lax.fori_loop(0, chf.shape[0] // 8, widen, 0)
+
+        def plane(i, _, g=g, j=j):
             z = g * zg + i
-            full = jnp.dot(basis_ref[...], ch_ref[z], preferred_element_type=jnp.float32)
+            here = chf[:, g * zg - j * part + i, :].astype(jnp.bfloat16)
+            full = jnp.dot(basis_ref[...], here, preferred_element_type=jnp.float32)
             at = 0
             for buf in (send1, keep):
                 for c in range(chunks):
@@ -144,26 +185,13 @@
         for c in range(chunks):
             l1(c, g).start()
 
-    for c in range(chunks):
-        errors = tuple(jnp.zeros((rows, cells), jnp.float32) for _ in range(nq - 1))
+        if g > 0:
+            errors = round_group(0, g - 1, errors)
+    round_group(0, groups - 1, errors)
+    for c in range(1, chunks):
+        errors = no_errors
         for g in range(groups):
-            l1(c, g).wait_recv()
-
-            def plane(i, errors, g=g, c=c):
-                z = g * zg + i
-                left = []
-                for d in range(1, nq):
-                    q = quad(d)
-                    v = keep[c, q, z] + recv1[c, q, z] + errors[d - 1]
-                    b = v.astype(jnp.bfloat16)
-                    l2send[c, d - 1, z] = b
-                    left.append(v - b.astype(jnp.float32))
-                srcx[c, h + z] = keep[c, p, z] + recv1[c, p, z]
-                return tuple(left)
-
-            errors = lax.fori_loop(0, zg, plane, errors, unroll=True)
-            for d in range(1, nq):
-                l2(c, g, d).start()
+            errors = round_group(c, g, errors)
 
     halo_wait_recv(*open_args)
 
@@ -181,8 +209,11 @@
         o = openx[pl.ds(z, count)]
         return jnp.concatenate([o] * (rows // 8), 1)
 
-    for c in range(chunks):
-        def gather_source(i, _, c=c):
+    def halo_of(c):
+        return (srcx.at[c], h, srcx.at[c], ha_s.at[c], ha_r.at[c])
+
+    def sources(c):
+        def gather_source(i, _):
             s = srcx[c, h + i]
             for d in range(1, nq):
                 s = s + l2recv[c, d - 1, i].astype(jnp.float32)
@@ -193,10 +224,11 @@
             for d in range(1, nq):
                 l2(c, g, d).wait_recv()
             lax.fori_loop(g * zg, (g + 1) * zg, gather_source, 0, unroll=True)
-        halo_args = (srcx.at[c], h, srcx.at[c], ha_s.at[c], ha_r.at[c])
-        halo_send(*halo_args)
-        halo_wait_recv(*halo_args)
-        halo_wait_send(*halo_args)
+        halo_send(*halo_of(c))
+
+    sources(0)
+    for c in range(chunks):
+        halo_wait_recv(*halo_of(c))
         inv = inv_ref[c]
 
         def begin(i, _, c=c, inv=inv):
@@ -233,6 +265,8 @@
         tot[c] = lax.fori_loop(0, depth, suffix, jnp.zeros((rows, cells), jnp.float32), unroll=8)
         for d in range(1, ngz):
             total(c, d).start()
+        if c + 1 < chunks:
+            sources(c + 1)
         before = jnp.zeros((rows, cells), jnp.float32)
         for d in range(1, ngz):
             total(c, d).wait_recv()
@@ -256,6 +290,7 @@
             forward(c, d).start()
     for c in range(chunks):
         gather_sib(c).wait()
+        halo_wait_send(*halo_of(c))
         for d in range(1, nq):
             gather(c, d).wait_send()
             forward(c, d).wait()
@@ -268,8 +303,9 @@
     halo_wait_send(*open_args)
 
 
-def synthesize(weight_ref, shift_ref, out_ref, wide_ref):
+def synthesize(weight_ref, shift_ref, pot_ref, out_ref, turned_ref, wide_ref):
     for z in range(shift_ref.shape[0]):
+        turned_ref[:, z, :] = pot_ref[z]
         wide_ref[:, z, :] = jnp.dot(
             weight_ref[...], shift_ref[z], preferred_element_type=jnp.float32
         )
@@ -290,7 +326,7 @@
     mode_rows = MODES // n
     rows = 16 if mode_rows % 16 == 0 else mode_rows
     chunks = mode_rows // rows
-    groups = 4
+    groups, part = 4, 16
     me = lax.axis_index("phi")
     core = me % 2
 
@@ -334,9 +370,12 @@
             jax.ShapeDtypeStruct((depth, mode_rows, cells), f32),
             jax.ShapeDtypeStruct((depth, MODES, cells), bf16),
         ),
-        in_specs=[vmem] * 5,
+        in_specs=[vmem, pl.BlockSpec(memory_space=pl.ANY)] + [vmem] * 3,
         out_specs=(vmem, vmem),
         scratch_shapes=[
+            pltpu.VMEM((depth // part, phi_rows, part, cells), bf16),
+            pltpu.VMEM((phi_rows, part, cells), f32),
+            sem((depth // part,)),
             pltpu.VMEM((chunks, nq, depth, rows, cells), f32),
             pltpu.VMEM((chunks, nq, depth, rows, cells), f32),
             pltpu.VMEM((chunks, nq, depth, rows, cells), f32),
@@ -362,22 +401,28 @@
         compiler_params=pltpu.CompilerParams(
             collective_id=0, has_side_effects=True, vmem_limit_bytes=48 * 1024 * 1024
         ),
-    )(basis, charge.transpose(1, 0, 2), open_cells, inv, coef)
-
-    part = 16
-    distortion = pl.pallas_call(
+    )(basis, charge, open_cells, inv, coef)
+
+    distortion, potential = pl.pallas_call(
         synthesize,
         grid=(depth // part,),
-        out_shape=jax.ShapeDtypeStruct((phi_rows, depth, cells), bf16),
+        out_shape=(
+            jax.ShapeDtypeStruct((phi_rows, depth, cells), bf16),
+            jax.ShapeDtypeStruct((mode_rows, depth, cells), f32),
+        ),
         in_specs=[
             pl.BlockSpec((phi_rows, MODES), lambda i: (0, 0)),
             pl.BlockSpec((part, MODES, cells), lambda i: (i, 0, 0)),
+            pl.BlockSpec((part, mode_rows, cells), lambda i: (i, 0, 0)),
         ],
-        out_specs=pl.BlockSpec((phi_rows, part, cells), lambda i: (0, i, 0)),
+        out_specs=(
+            pl.BlockSpec((phi_rows, part, cells), lambda i: (0, i, 0)),
+            pl.BlockSpec((mode_rows, part, cells), lambda i: (0, i, 0)),
+        ),
         scratch_shapes=[pltpu.VMEM((phi_rows, part, cells), f32)],
         compiler_params=pltpu.CompilerParams(vmem_limit_bytes=32 * 1024 * 1024),
-    )(table.T, shifts)
-    return (distortion, potential.transpose(1, 0, 2))
+    )(table.T, shifts, potential)
+    return (distortion, potential)
 
 
 def solution(mesh):

time: 60.5 us -> 54.3 us (0.90)
  local copies, waits for them, and re-layouts: 8.37 us -> 0.22 us
  Pallas kernels: 47.9 us -> 49.9 us
    unnamed x2 -> x0, local copies, waits for them, and re-layouts: 8.15 us -> none
    pallas_call x1, Pallas kernels: 42.4 us -> 43.6 us  [on_device(): pl.pallas_call(functools.partial(kernel, n, ngz, chunks, groups), out_sha...]
    pallas_call x1, Pallas kernels: 5.53 us -> 6.36 us  [on_device(): pl.pallas_call(synthesize, grid=(depth // part,), out_shape=(jax.ShapeDty...]
where the time goes in v3:
time: 54.3 us; the launch traced here: 54.1 us
  Pallas kernels  49.9 us (92%)
  other arithmetic  3.19 us (6%)
  between operations  0.74 us (1%)
    pallas_call x1, Pallas kernels, on_device(): pl.pallas_call(functools.partial(kernel, n, ngz, chunks, groups), out_sha...  43.6 us
    pallas_call x1, Pallas kernels, on_device(): pl.pallas_call(synthesize, grid=(depth // part,), out_shape=(jax.ShapeDty...  6.36 us
    cos x1, other arithmetic, on_device(): jnp.cos(angles)  1.25 us

profile of v3, /device:TPU:0, one launch (start us, length us, event | category | flops | bytes accessed | tf_op | source)
XLA Modules:
  0.0 54.1 jit_solution(11093688081791763790)
XLA Ops:
  0.7 0.8 %select_reduce_fusion = s32[32]{0:T(128)S(1)} fusion(s32[64]{0:T(128)} %param.4, s32[32]{0:T(128)S(1)} %and_select_fusion), kind=kLoop, calls=%fused_computation.17 | loop fusion | flops 6112 | bytes 512 | tf_op jit(solution)/shard_map/reduce_sum | solution.py:343
  1.5 0.1 convert_element_type.51
  1.7 0.1 fusion.7.inv_ref
  1.8 0.8 %subtract_convert_fusion = f32[32,256]{1,0:T(8,128)S(1)} fusion(s32[32,256]{1,0:T(8,128)} %param.5), kind=kLoop, calls=%fused_computation.16 | loop fusion | flops 16384 | bytes 65536 | tf_op jit(solution)/shard_map/convert_element_type | solution.py:359
  2.5 1.2 %fusion.5 = (bf16[64,256]{0,1:T(8,128)(2,1)S(1)}, bf16[64,256]{0,1:T(8,128)(2,1)S(1)}) fusion(s32[256]{0:T(256)S(1)} %iota_add_fusion, s32[64]{0:T(128)} %param.4), kind=kLoop, calls=%fused_computation.12 | loop fusion | flops 262144 | bytes 66816 | tf_op jit(solution)/shard_map/cos | solution.py:336
  3.8 0.1 fusion.9.weight_ref
  3.9 0.1 maximum_convert_fusion
  4.0 0.1 copy.8
  4.1 43.6 %shard_map.50 = (f32[32,32,256]{2,1,0:T(8,128)S(1)}, bf16[32,128,256]{2,1,0:T(8,128)(2,1)S(1)}) custom-call(bf16[128,256]{1,0:T(8,128)(2,1)S(1)} %bitcast.6, bf16[256,32,256]{2,1,0:T(8,128)(2,1)} %charge_ref.1, f32[32,8,256]{2,1,0:T(8,128)S(1)} %broadcast_in_dim.16.open_ref, f32[2,16,256]{2,1,0:T(8,128)S(1)} %fusion.7.inv_ref, ...), custom_call_target="tpu_custom_call" | custom-call | tf_op jit(solution)/shard_map/pallas_call | solution.py:367
  47.7 6.4 %shard_map.51 = (bf16[256,32,256]{2,1,0:T(8,128)(2,1)}, f32[32,32,256]{2,1,0:T(8,128)}) custom-call(bf16[256,128]{1,0:T(8,128)(2,1)S(1)} %fusion.9.weight_ref, bf16[32,128,256]{2,1,0:T(8,128)(2,1)S(1)} %get-tuple-element.4.shift_ref, f32[32,32,256]{2,1,0:T(8,128)S(1)} %get-tuple-element.5.pot_ref), custom_call_target="tpu_custom_call" | custom-call | tf_op jit(solution)/shard_map/pallas_call | solution.py:406
  (11 shorter events, 0.1 us)

commit v4 on v3

--- a/solution.py
+++ b/solution.py
@@ -131,9 +131,7 @@
     def _():
         no_slab(h + depth)
 
-    pl.semaphore_wait(barrier, nq + ngz - 1)
     open_args = (open_ref, 0, openx, op_s, op_r)
-    halo_send(*open_args)
 
     def round_group(c, g, errors):
         l1(c, g).wait_recv()
@@ -182,6 +180,9 @@
             return 0
 
         lax.fori_loop(0, zg, plane, 0, unroll=True)
+        if g == 0:
+            pl.semaphore_wait(barrier, nq + ngz - 1)
+            halo_send(*open_args)
         for c in range(chunks):
             l1(c, g).start()
 
@@ -338,9 +339,8 @@
     swapped = jnp.where(core == 0, blocks[:, ::-1], blocks)
     basis = swapped.transpose(1, 2, 0, 3, 4).reshape(MODES, phi_rows)
 
-    mode_ids = me * mode_rows + jnp.arange(mode_rows, dtype=jnp.int32)
-    matches = mode_ids[:, None] % ORDERS == jnp.arange(ORDERS, dtype=jnp.int32)[None, :]
-    values = jnp.sum(jnp.where(matches, orders[None, :], 0), 1).astype(jnp.float32)
+    twice = jnp.concatenate([orders, orders])
+    values = lax.dynamic_slice_in_dim(twice, me * mode_rows, mode_rows).astype(jnp.float32)
     cell = jnp.arange(cells, dtype=jnp.int32)
     radius = cell.astype(jnp.float32) + (cells // 2 + 0.5)
     inv = 1.0 / (4.0 + (values[:, None] / radius[None, :]) ** 2)

time: 54.3 us -> 53.4 us (0.983)
  Pallas kernels: 49.9 us -> 49 us
    pallas_call x1, Pallas kernels: 43.6 us -> 42.6 us  [on_device(): pl.pallas_call(functools.partial(kernel, n, ngz, chunks, groups), out_sha...]
    reduce_sum x1 -> x0, other arithmetic: 0.84 us -> none  [on_device(): jnp.sum(jnp.where(matches, orders[None, :], 0), 1).astype(jnp.float32)]
    concatenate x0 -> x1, other arithmetic: none -> 0.81 us  [on_device(): twice = jnp.concatenate([orders, orders])]
where the time goes in v4:
time: 53.4 us; the launch traced here: 53.2 us
  Pallas kernels  49 us (92%)
  other arithmetic  3.22 us (6%)
  between operations  0.73 us (1%)
    pallas_call x1, Pallas kernels, on_device(): pl.pallas_call(functools.partial(kernel, n, ngz, chunks, groups), out_sha...  42.6 us
    pallas_call x1, Pallas kernels, on_device(): pl.pallas_call(synthesize, grid=(depth // part,), out_shape=(jax.ShapeDty...  6.36 us
    cos x1, other arithmetic, on_device(): jnp.cos(angles)  1.25 us

profile of v4, /device:TPU:0, one launch (start us, length us, event | category | flops | bytes accessed | tf_op | source)
XLA Modules:
  0.0 53.2 jit_solution(13442274888182245103)
XLA Ops:
  0.6 0.8 %pad_add_fusion = s32[128]{0:T(128)S(1)} fusion(s32[64]{0:T(128)} %param.4), kind=kLoop, calls=%fused_computation.25 | loop fusion | flops 128 | bytes 768 | tf_op jit(solution)/shard_map/concatenate | solution.py:342
  1.4 0.1 dynamic-slice_convert_fusion
  1.5 0.1 div.41
  1.7 0.1 fusion.7.inv_ref
  1.8 0.8 %subtract_convert_fusion = f32[32,256]{1,0:T(8,128)S(1)} fusion(s32[32,256]{1,0:T(8,128)} %param.5), kind=kLoop, calls=%fused_computation.16 | loop fusion | flops 16384 | bytes 65536 | tf_op jit(solution)/shard_map/convert_element_type | solution.py:359
  2.5 1.2 %fusion.5 = (bf16[64,256]{0,1:T(8,128)(2,1)S(1)}, bf16[64,256]{0,1:T(8,128)(2,1)S(1)}) fusion(s32[256]{0:T(256)S(1)} %iota_add_fusion, s32[64]{0:T(128)} %param.4), kind=kLoop, calls=%fused_computation.12 | loop fusion | flops 262144 | bytes 66816 | tf_op jit(solution)/shard_map/cos | solution.py:337
  3.8 0.1 fusion.8.weight_ref
  3.9 0.1 maximum_convert_fusion
  4.0 0.1 copy.6
  4.2 42.6 %shard_map.50 = (f32[32,32,256]{2,1,0:T(8,128)S(1)}, bf16[32,128,256]{2,1,0:T(8,128)(2,1)S(1)}) custom-call(bf16[128,256]{1,0:T(8,128)(2,1)S(1)} %bitcast.6, bf16[256,32,256]{2,1,0:T(8,128)(2,1)} %charge_ref.1, f32[32,8,256]{2,1,0:T(8,128)S(1)} %broadcast_in_dim.4.open_ref, f32[2,16,256]{2,1,0:T(8,128)S(1)} %fusion.7.inv_ref, ...), custom_call_target="tpu_custom_call" | custom-call | tf_op jit(solution)/shard_map/pallas_call | solution.py:367
  46.8 6.4 %shard_map.51 = (bf16[256,32,256]{2,1,0:T(8,128)(2,1)}, f32[32,32,256]{2,1,0:T(8,128)}) custom-call(bf16[256,128]{1,0:T(8,128)(2,1)S(1)} %fusion.8.weight_ref, bf16[32,128,256]{2,1,0:T(8,128)(2,1)S(1)} %get-tuple-element.4.shift_ref, f32[32,32,256]{2,1,0:T(8,128)S(1)} %get-tuple-element.5.pot_ref), custom_call_target="tpu_custom_call" | custom-call | tf_op jit(solution)/shard_map/pallas_call | solution.py:406
  (9 shorter events, 0.1 us)
